TPU v7x, 256 devices: a whole 4x4x8 slice. The times are simulated.
256 devices in a mesh: wide: 16 (over z, core), grow: 4 (over y), gcol: 4 (over x).
Axes of the slice: x: 4, y: 4, z: 8, core: 2. Of those that a mesh axis runs over, the one named last changes fastest.
Arguments:
- diag_block: float32 [16, 1024, 1024], P('wide', ('grow', 'gcol')), as said below
- lower_block: float32 [16, 3072, 1024], P('wide', ('grow', 'gcol')), may hold values from -0.1875 to 0.1875
- trailing_block: float32 [16, 3072, 3072], P('wide', 'grow', 'gcol'), as said below
- parent_front: float32 [4, 2048, 8192], P('grow', 'wide', 'gcol'), may hold values from -3 to 3
- row_map: int32 [16, 24], replicated, may hold values from 0 to 63, as said below
Outputs:
- factor: float32 [16, 1024, 1024], P('wide', ('grow', 'gcol'))
- panel: float32 [16, 3072, 1024], P('wide', ('grow', 'gcol'))
- parent: float32 [4, 2048, 8192], P('grow', 'wide', 'gcol')
Inputs may be any that keep to these rules, and one draw needn't show every extreme that they name: Each diag_block[g] is symmetric and positive definite. Each trailing_block[g] is symmetric. `row_map`: the blocks of one child are distinct, and child block b goes to a grandparent block p with p // 16 equal to b // 6.
All inputs are finite; a program needn't handle non-finite values.
Results may differ from a plain program's by a relative error of at most 0.0003.
Values sent between devices are 32-bit elements; how exact they have to be, the bound alone decides.
No kernel may reach another device: no remote copies, remote signals or barrier semaphores. Data moves between devices by JAX's collectives and lax.ppermute only.
A program may use at most 128 MiB of HBM per device.

v0:
```python
import jax
import jax.numpy as jnp
from jax import lax
from jax.sharding import PartitionSpec as P

BLOCK = 128


def cut_rows(length, count):
    unit = 8 if length >= 8 * count else 1
    return [length // unit * k // count * unit for k in range(1, count)]


def gather_in_order(x, axes, turns):
    tiles = x
    for k in turns:
        tiles = lax.all_gather(tiles, axes[k])
    done = turns[::-1]
    back = [done.index(k) for k in range(len(axes))]
    tiles = tiles.transpose(*back, *range(len(axes), tiles.ndim))
    return tiles.reshape(-1, *x.shape)


def laid_out(tiles, dim):
    dims = list(tiles.shape[1:])
    dims[dim] *= tiles.shape[0]
    return jnp.moveaxis(tiles, 0, dim).reshape(dims)


def gather_at_once(x, axes, dim):
    cut = max(range(max(1, x.ndim - 1)), key=lambda d: x.shape[d])
    count, gathered = (len(axes), [])
    for initial, section in enumerate(jnp.split(x, cut_rows(x.shape[cut], count), axis=cut)):
        if section.size:
            turns = [(initial - k) % count for k in range(count)]
            gathered.append(gather_in_order(section, axes, turns))
    return laid_out(jnp.concatenate(gathered, axis=cut + 1), dim)


def filled_up(lines, peers):
    spare = -lines.shape[0] % peers
    if not spare:
        return lines
    return jnp.concatenate([lines, jnp.zeros((spare, *lines.shape[1:]), lines.dtype)])


def broadcast_by_parts(x, axis, root):
    lines = jnp.where(lax.axis_index(axis) == root, x, jnp.zeros_like(x)).reshape(
        -1, *x.shape[1:][-1:]
    )
    padded = filled_up(lines, lax.axis_size(axis))
    own = lax.psum_scatter(padded, axis, scatter_dimension=0, tiled=True)
    return lax.all_gather(own, axis, axis=0, tiled=True)[: len(lines)].reshape(x.shape)


def local(diag_block, lower_block, trailing_block, parent_front, row_map):
    highest = lax.Precision.HIGHEST
    whole = gather_at_once(diag_block[0], ("grow", "gcol"), 0)
    factor = jnp.linalg.cholesky(whole)
    share = diag_block.shape[1]
    factor_rows = lax.dynamic_slice_in_dim(
        factor, lax.axis_index(("grow", "gcol")) * share, share, 0
    )
    panel = jax.scipy.linalg.solve_triangular(factor, lower_block[0].T, lower=True).T
    row_part = lax.all_gather(panel, "gcol", axis=0, tiled=True)
    column_index = lax.axis_index("gcol")
    col_part = broadcast_by_parts(row_part, "grow", column_index)
    update = lax.dot_general(
        row_part,
        col_part,
        (((1,), (1,)), ((), ())),
        precision=highest,
        preferred_element_type=jnp.float32,
    )
    schur = trailing_block[0] - update
    owners = lax.axis_size("wide")
    child = lax.axis_index("wide")
    row_index = lax.axis_index("grow")
    width_blocks = schur.shape[0] // BLOCK
    quarter_blocks = parent_front.shape[1] * owners // BLOCK
    column_blocks = parent_front.shape[2] // BLOCK
    row_local = (
        lax.dynamic_slice_in_dim(row_map, row_index * width_blocks, width_blocks, 1)
        % quarter_blocks
    )
    col_local = (
        lax.dynamic_slice_in_dim(row_map, column_index * width_blocks, width_blocks, 1)
        % column_blocks
    )
    grid = jnp.arange(column_blocks, dtype=jnp.int32)
    mine_rows = lax.dynamic_slice_in_dim(row_local, child, 1, 0)[0]
    mine_cols = lax.dynamic_slice_in_dim(col_local, child, 1, 0)[0]
    col_place = (mine_cols[None, :] == grid[:, None]).astype(jnp.float32)
    pieces = schur.reshape(width_blocks, BLOCK, width_blocks, BLOCK)
    count = parent_front.shape[1] * lax.axis_size("wide")
    blocks = count // BLOCK
    wanted = jnp.arange(blocks, dtype=jnp.int32)
    row_place = (mine_rows[None, :] == wanted[:, None]).astype(jnp.float32)
    placed = jnp.einsum("pb,bxcy->pxcy", row_place, pieces, precision=highest)
    spread = jnp.einsum("pxcy,qc->pxqy", placed, col_place, precision=highest)
    summed = lax.psum_scatter(
        spread.reshape(count, column_blocks * BLOCK), "wide", scatter_dimension=0, tiled=True
    )
    parent = parent_front + summed[None]
    return (factor_rows[None], panel[None], parent)


def solution(mesh):
    placed = (
        P("wide", ("grow", "gcol"), None),
        P("wide", ("grow", "gcol"), None),
        P("wide", "grow", "gcol"),
        P("grow", "wide", "gcol"),
        P(),
    )
    return jax.shard_map(
        local,
        mesh=mesh,
        in_specs=placed,
        out_specs=(
            P("wide", ("grow", "gcol"), None),
            P("wide", ("grow", "gcol"), None),
            P("grow", "wide", "gcol"),
        ),
        check_vma=False,
    )
```

profile of v0, /device:TPU:2, one launch (start us, length us, event | category | flops | bytes accessed | tf_op | source)
XLA Modules:
  0.0 715.4 jit_solution(11808410995972547139)
XLA Ops:
  8.2 14.0 %all_gather.26 = f32[4,32,1024]{2,1,0:T(8,128)} all-gather(f32[1,32,1024]{2,1,0:T(8,128)S(1)} %get-tuple-element.27), channel_id=1, replica_groups=mesh['wide'=16,'grow'=4,'gcol'=4] {'grow'}, dimensions={0}, use_global_device_ids=true | all-gather | bytes 655360 | tf_op jit(solution)/shard_map/all_gather | solution.py:17
  22.3 13.6 %all_gather.29 = f32[4,32,1024]{2,1,0:T(8,128)} all-gather(f32[1,32,1024]{2,1,0:T(8,128)S(1)} %get-tuple-element.28), channel_id=1, replica_groups=mesh['wide'=16,'grow'=4,'gcol'=4] {'gcol'}, dimensions={0}, use_global_device_ids=true | all-gather | bytes 655360 | tf_op jit(solution)/shard_map/all_gather | solution.py:17
  36.0 21.8 %all-gather.11.cloned.1.call-done = f32[16,32,1024]{2,1,0:T(8,128)} async-done(((f32[4,32,1024]{2,1,0:T(8,128)}), f32[16,32,1024]{2,1,0:T(8,128)}) %all-gather.11.cloned.1.call-update) | async-done | bytes 2097168 | tf_op jit(solution)/shard_map/all_gather | solution.py:17
  59.5 34.5 %all-gather.13.cloned.1.call-done = f32[16,32,1024]{2,1,0:T(8,128)} async-done(((f32[4,32,1024]{2,1,0:T(8,128)}), f32[16,32,1024]{2,1,0:T(8,128)}) %all-gather.13.cloned.1.call-update) | async-done | bytes 2097168 | tf_op jit(solution)/shard_map/all_gather | solution.py:17
  109.8 11.7 %cholesky.223 = f32[128,128]{1,0:T(8,128)S(1)} custom-call(f32[128,128]{1,0:T(8,128)S(1)} %cholesky.580), custom_call_target="Cholesky" | custom-call | tf_op jit(solution)/shard_map/jit(cholesky)/cholesky | solution.py:59
  121.5 9.8 %custom-call.63 = f32[1,128,128]{1,2,0:T(8,128)S(1)} custom-call(f32[1,128,128]{2,1,0:T(8,128)S(1)} %get-tuple-element.75), custom_call_target="InvertDiagBlocksLowerTriangular" | custom-call | tf_op jit(solution)/shard_map/jit(cholesky)/cholesky | solution.py:59
  137.8 11.9 %cholesky.244 = f32[128,128]{1,0:T(8,128)S(1)} custom-call(f32[128,128]{1,0:T(8,128)S(1)} %cholesky.584), custom_call_target="Cholesky" | custom-call | tf_op jit(solution)/shard_map/jit(cholesky)/cholesky | solution.py:59
  163.5 11.7 %cholesky.468 = f32[128,128]{1,0:T(8,128)S(1)} custom-call(f32[128,128]{1,0:T(8,128)S(1)} %cholesky.589), custom_call_target="Cholesky" | custom-call | tf_op jit(solution)/shard_map/jit(cholesky)/cholesky | solution.py:59
  189.8 11.9 %cholesky.487 = f32[128,128]{1,0:T(8,128)S(1)} custom-call(f32[128,128]{1,0:T(8,128)S(1)} %cholesky.594), custom_call_target="Cholesky" | custom-call | tf_op jit(solution)/shard_map/jit(cholesky)/cholesky | solution.py:59
  203.0 9.8 %custom-call.66 = f32[1,128,128]{1,2,0:T(8,128)S(1)} custom-call(f32[1,128,128]{2,1,0:T(8,128)S(1)} %get-tuple-element.66), custom_call_target="InvertDiagBlocksLowerTriangular" | custom-call | tf_op jit(solution)/shard_map/jit(cholesky)/cholesky | solution.py:59
  216.2 11.7 %cholesky.506 = f32[128,128]{1,0:T(8,128)S(1)} custom-call(f32[128,128]{1,0:T(8,128)S(1)} %cholesky.599), custom_call_target="Cholesky" | custom-call | tf_op jit(solution)/shard_map/jit(cholesky)/cholesky | solution.py:59
  229.2 10.2 %custom-call.67 = f32[1,128,128]{1,2,0:T(8,128)S(1)} custom-call(f32[1,128,128]{2,1,0:T(8,128)S(1)} %get-tuple-element.63), custom_call_target="InvertDiagBlocksLowerTriangular" | custom-call | tf_op jit(solution)/shard_map/jit(cholesky)/cholesky | solution.py:59
  242.8 11.7 %cholesky.526 = f32[128,128]{1,0:T(8,128)S(1)} custom-call(f32[128,128]{1,0:T(8,128)S(1)} %cholesky.604), custom_call_target="Cholesky" | custom-call | tf_op jit(solution)/shard_map/jit(cholesky)/cholesky | solution.py:59
  268.5 11.9 %cholesky.546 = f32[128,128]{1,0:T(8,128)S(1)} custom-call(f32[128,128]{1,0:T(8,128)S(1)} %cholesky.609), custom_call_target="Cholesky" | custom-call | tf_op jit(solution)/shard_map/jit(cholesky)/cholesky | solution.py:59
  294.1 11.7 %cholesky.564 = f32[128,128]{1,0:T(8,128)S(1)} custom-call(f32[128,128]{1,0:T(8,128)S(1)} %convolution_subtract_fusion.13), custom_call_target="Cholesky" | custom-call | tf_op jit(solution)/shard_map/jit(cholesky)/cholesky | solution.py:59
  319.5 23.2 %while.1 = (s32[]{:T(128)}, f32[1024,1024]{1,0:T(8,128)}, s32[8,2]{0,1:T(2,128)S(1)}, f32[8,128,128]{2,1,0:T(8,128)S(1)}, s32[]{:T(128)}) while((s32[]{:T(128)}, f32[1024,1024]{1,0:T(8,128)}, s32[8,2]{0,1:T(2,128)S(1)}, f32[8,128,128]{2,1,0:T(8,128)S(1)}, s32[]{:T(128)}) %tuple.67), condition=%wide.while_cond, body=%wide.while_body.sunk | while | flops 2 | bytes 131189 | solution.py:64
  342.7 78.8 %custom-call.70 = f32[8,128,128]{1,2,0:T(8,128)S(1)} custom-call(f32[8,128,128]{2,1,0:T(8,128)S(1)} %get-tuple-element.10), custom_call_target="InvertDiagBlocksLowerTriangular" | custom-call | tf_op jit(solution)/shard_map/jit(_solve_triangular)/triangular_solve | solution.py:64
  434.6 41.4 %all-gather.7.cloned.1.call-done = f32[768,1024]{1,0:T(8,128)} async-done(((f32[192,1024]{1,0:T(8,128)}), f32[768,1024]{1,0:T(8,128)}) %all-gather.7.cloned.1.call-update) | async-done | bytes 3145744 | tf_op jit(solution)/shard_map/all_gather | solution.py:65
  478.4 44.0 %reduce-scatter.3.cloned.1.call-done = f32[192,1024]{1,0:T(8,128)} async-done(((f32[768,1024]{1,0:T(8,128)}), f32[192,1024]{1,0:T(8,128)}) %reduce-scatter.3.cloned.1.call-update) | async-done | bytes 786448 | tf_op jit(solution)/shard_map/reduce_scatter | solution.py:52
  522.5 43.4 %all-gather.9.cloned.1.call-done = f32[768,1024]{1,0:T(8,128)} async-done(((f32[192,1024]{1,0:T(8,128)}), f32[768,1024]{1,0:T(8,128)}) %all-gather.9.cloned.1.call-update) | async-done | bytes 3145744 | tf_op jit(solution)/shard_map/all_gather | solution.py:53
  565.9 11.4 %bitcast_subtract_fusion = f32[768,768]{1,0:T(8,128)} fusion(f32[1,768,768]{2,1,0:T(8,128)} %param.7, f32[768,1024]{1,0:T(8,128)S(1)} %copy-done, f32[768,1024]{1,0:T(8,128)} %all-gather.9.cloned.1.call-done), kind=kOutput, calls=%fused_computation.13 | convolution fusion | flops 7248347136 | bytes 11010048 | tf_op jit(solution)/shard_map/dot_general | solution.py:68
  583.8 9.9 %fusion = f32[16,16,128,128]{3,0,2,1:T(8,128)S(1)} fusion(f32[16,128,6,128]{3,0,2,1:T(8,128)S(1)} %fusion.4, s32[6]{0:T(128)S(1)} %fusion.71), kind=kOutput, calls=%fused_computation.3 | convolution fusion | flops 301989984 | bytes 23068696 | tf_op jit(solution)/shard_map/pxcy,qc->pxqy/dot_general | solution.py:100
  593.7 11.2 %copy.25 = f32[256,8,16,128]{3,1,2,0:T(8,128)} copy(f32[256,8,16,128]{3,2,1,0:T(8,128)S(1)} %bitcast.141) | data formatting | bytes 33554432
  606.7 99.1 %reduce-scatter.5.cloned.1.call-done = f32[128,2048]{1,0:T(8,128)} async-done(((f32[2048,2048]{1,0:T(8,128)}), f32[128,2048]{1,0:T(8,128)}) %reduce-scatter.5.cloned.1.call-update) | async-done | bytes 1048592 | tf_op jit(solution)/shard_map/reduce_scatter | solution.py:101
  (121 shorter events, 148.4 us)
Async XLA Ops:
  7.2 50.6 %all-gather.11.cloned.1.call-start = ((), (), s32[]{:S(2)}) async-start(), calls=%async_computation.6 | async-start | bytes 2621440 | tf_op jit(solution)/shard_map/all_gather | solution.py:17
  22.3 71.7 %all-gather.13.cloned.1.call-start = ((), (), s32[]{:S(2)}) async-start(), calls=%async_computation.7 | async-start | bytes 2621440 | tf_op jit(solution)/shard_map/all_gather | solution.py:17
  35.9 440.1 %all-gather.7.cloned.1.call-start = ((), (), s32[]{:S(2)}) async-start(), calls=%async_computation.2 | async-start | bytes 3932160 | tf_op jit(solution)/shard_map/all_gather | solution.py:65
  107.9 1.9 copy-start.1
  312.8 108.7 %copy-start.4 = (f32[1,192,1024]{2,1,0:T(8,128)S(1)}, f32[1,192,1024]{2,1,0:T(8,128)}, u32[]{:S(2)}) copy-start(f32[1,192,1024]{2,1,0:T(8,128)} %param.6) | copy-start | bytes 2359300
  433.6 0.9 copy-start.3
  434.6 87.8 %reduce-scatter.3.cloned.1.call-start = ((), (), s32[]{:S(2)}) async-start(), calls=%async_computation.3 | async-start | bytes 3932160 | tf_op jit(solution)/shard_map/reduce_scatter | solution.py:52
  434.6 87.8 %copy-start.5 = (s32[16,24]{1,0:T(8,128)S(1)}, s32[16,24]{1,0:T(8,128)}, u32[]{:S(2)}) copy-start(s32[16,24]{1,0:T(8,128)} %param.9) | copy-start | bytes 4612
  476.0 89.9 %copy-start = (f32[768,1024]{1,0:T(8,128)S(1)}, f32[768,1024]{1,0:T(8,128)}, u32[]{:S(2)}) copy-start(f32[768,1024]{1,0:T(8,128)} %all-gather.7.cloned.1.call-done) | copy-start | bytes 9437188
  478.3 87.6 %all-gather.9.cloned.1.call-start = ((), (), s32[]{:S(2)}) async-start(), calls=%async_computation.4 | async-start | bytes 3932160 | tf_op jit(solution)/shard_map/all_gather | solution.py:53
  522.3 183.5 %reduce-scatter.5.cloned.1.call-start = ((), (), s32[]{:S(2)}) async-start(), calls=%async_computation.5 | async-start | bytes 17825792 | tf_op jit(solution)/shard_map/reduce_scatter | solution.py:101
  604.9 100.9 %copy-start.2 = (f32[1,128,2048]{2,1,0:T(8,128)S(1)}, f32[1,128,2048]{2,1,0:T(8,128)}, u32[]{:S(2)}) copy-start(f32[1,128,2048]{2,1,0:T(8,128)} %param.8) | copy-start | bytes 3145732
Sparse Core Ops, SparseCore 0:
  22.4 35.3 all-gather.10
  59.6 34.4 all-gather.12
  434.7 41.3 all-gather.6
  478.4 43.8 reduce-scatter.2
  524.0 41.8 all-gather.8
  605.1 100.7 reduce-scatter.4
where the time goes:
time: 726 us; the launch traced here: 715 us
  waiting for transfers between devices  284 us (39%)
  other arithmetic  271 us (37%)
  matrix products  60.4 us (8%)
  local copies, waits for them, and re-layouts  51.9 us (7%)
  blocking collectives  27.6 us (4%)
  between operations  20 us (3%)
    another operation x30, other arithmetic, local(): factor = jnp.linalg.cholesky(whole)  172 us
    reduce_scatter x1, waiting for transfers between devices, local(): lax.psum_scatter(spread.reshape(count, column_blocks * BLOCK), 'wide', sc...  99.1 us
    another operation x3, other arithmetic, local(): jax.scipy.linalg.solve_triangular(factor, lower_block[0].T, lower=True)  85.5 us
    all_gather x2, waiting for transfers between devices, gather_in_order(): tiles = lax.all_gather(tiles, axes[k])  56.3 us
    reduce_scatter x1, waiting for transfers between devices, broadcast_by_parts(): own = lax.psum_scatter(padded, axis, scatter_dimension=0, tiled=True)  44 us
    all_gather x1, waiting for transfers between devices, broadcast_by_parts(): lax.all_gather(own, axis, axis=0, tiled=True)[:len(lines)].reshape(x.shape)  43.4 us
    all_gather x1, waiting for transfers between devices, local(): row_part = lax.all_gather(panel, 'gcol', axis=0, tiled=True)  41.4 us
    all_gather x2, blocking collectives, gather_in_order(): tiles = lax.all_gather(tiles, axes[k])  27.6 us
  transfers between devices with their start and end apart: 6, of which 6 were waited for; matrix products, arithmetic and copies ran while one was open for 1% of the time, Pallas kernels for 0%

commit v1 on v0

--- a/solution.py
+++ b/solution.py
@@ -62,7 +62,12 @@
         factor, lax.axis_index(("grow", "gcol")) * share, share, 0
     )
     panel = jax.scipy.linalg.solve_triangular(factor, lower_block[0].T, lower=True).T
-    row_part = lax.all_gather(panel, "gcol", axis=0, tiled=True)
+    ring = [panel]
+    for hop in range(3):
+        ring.append(lax.ppermute(ring[-1], "gcol", [(dev, (dev + 1) % 4) for dev in range(4)]))
+    row_part = jnp.roll(
+        jnp.concatenate(ring[::-1], axis=0), (lax.axis_index("gcol") + 1) * ring[0].shape[0], axis=0
+    )
     column_index = lax.axis_index("gcol")
     col_part = broadcast_by_parts(row_part, "grow", column_index)
     update = lax.dot_general(

time: 726 us -> 740 us (1.019)
  waiting for transfers between devices: 284 us -> 292 us
    ppermute x0 -> x3, waiting for transfers between devices: none -> 52.1 us  [local(): lax.ppermute(ring[-1], 'gcol', [(dev, (dev + 1) % 4) for dev in range(4)])]
    all_gather x1 -> x0, waiting for transfers between devices: 41.4 us -> none  [local(): row_part = lax.all_gather(panel, 'gcol', axis=0, tiled=True)]
    unnamed x13 -> x22, local copies, waits for them, and re-layouts: 14 us -> 16.2 us
  transfers between devices with their start and end apart: 6 -> 8, of which waited for: 6 -> 8; matrix products, arithmetic and copies ran while one was open for 1% -> 0% of each run, Pallas kernels for 0% -> 0%
where the time goes in v1:
time: 740 us; the launch traced here: 730 us
  waiting for transfers between devices  292 us (39%)
  other arithmetic  271 us (37%)
  matrix products  60.7 us (8%)
  local copies, waits for them, and re-layouts  54.2 us (7%)
  blocking collectives  27.6 us (4%)
  between operations  19.7 us (3%)
    another operation x30, other arithmetic, local(): factor = jnp.linalg.cholesky(whole)  172 us
    reduce_scatter x1, waiting for transfers between devices, local(): lax.psum_scatter(spread.reshape(count, column_blocks * BLOCK), 'wide', sc...  99.1 us
    another operation x3, other arithmetic, local(): jax.scipy.linalg.solve_triangular(factor, lower_block[0].T, lower=True)  85.5 us
    all_gather x2, waiting for transfers between devices, gather_in_order(): tiles = lax.all_gather(tiles, axes[k])  56.3 us
    ppermute x3, waiting for transfers between devices, local(): lax.ppermute(ring[-1], 'gcol', [(dev, (dev + 1) % 4) for dev in range(4)])  52.1 us
    all_gather x1, waiting for transfers between devices, broadcast_by_parts(): lax.all_gather(own, axis, axis=0, tiled=True)[:len(lines)].reshape(x.shape)  43.3 us
    reduce_scatter x1, waiting for transfers between devices, broadcast_by_parts(): own = lax.psum_scatter(padded, axis, scatter_dimension=0, tiled=True)  40.9 us
    all_gather x2, blocking collectives, gather_in_order(): tiles = lax.all_gather(tiles, axes[k])  27.6 us
  transfers between devices with their start and end apart: 8, of which 8 were waited for; matrix products, arithmetic and copies ran while one was open for 0% of the time, Pallas kernels for 0%

profile of v1, /device:TPU:2, one launch (start us, length us, event | category | flops | bytes accessed | tf_op | source)
XLA Modules:
  0.0 729.6 jit_solution(18411247549285595530)
XLA Ops:
  8.2 14.0 %all_gather.23 = f32[4,32,1024]{2,1,0:T(8,128)} all-gather(f32[1,32,1024]{2,1,0:T(8,128)S(1)} %get-tuple-element.27), channel_id=1, replica_groups=mesh['wide'=16,'grow'=4,'gcol'=4] {'grow'}, dimensions={0}, use_global_device_ids=true | all-gather | bytes 655360 | tf_op jit(solution)/shard_map/all_gather | solution.py:17
  22.3 13.6 %all_gather.26 = f32[4,32,1024]{2,1,0:T(8,128)} all-gather(f32[1,32,1024]{2,1,0:T(8,128)S(1)} %get-tuple-element.28), channel_id=1, replica_groups=mesh['wide'=16,'grow'=4,'gcol'=4] {'gcol'}, dimensions={0}, use_global_device_ids=true | all-gather | bytes 655360 | tf_op jit(solution)/shard_map/all_gather | solution.py:17
  36.0 21.8 %all-gather.8.cloned.1.call-done = f32[16,32,1024]{2,1,0:T(8,128)} async-done(((f32[4,32,1024]{2,1,0:T(8,128)}), f32[16,32,1024]{2,1,0:T(8,128)}) %all-gather.8.cloned.1.call-update) | async-done | bytes 2097168 | tf_op jit(solution)/shard_map/all_gather | solution.py:17
  59.5 34.5 %all-gather.10.cloned.1.call-done = f32[16,32,1024]{2,1,0:T(8,128)} async-done(((f32[4,32,1024]{2,1,0:T(8,128)}), f32[16,32,1024]{2,1,0:T(8,128)}) %all-gather.10.cloned.1.call-update) | async-done | bytes 2097168 | tf_op jit(solution)/shard_map/all_gather | solution.py:17
  109.8 11.7 %cholesky.223 = f32[128,128]{1,0:T(8,128)S(1)} custom-call(f32[128,128]{1,0:T(8,128)S(1)} %cholesky.580), custom_call_target="Cholesky" | custom-call | tf_op jit(solution)/shard_map/jit(cholesky)/cholesky | solution.py:59
  137.8 12.0 %cholesky.244 = f32[128,128]{1,0:T(8,128)S(1)} custom-call(f32[128,128]{1,0:T(8,128)S(1)} %cholesky.584), custom_call_target="Cholesky" | custom-call | tf_op jit(solution)/shard_map/jit(cholesky)/cholesky | solution.py:59
  163.6 11.7 %cholesky.468 = f32[128,128]{1,0:T(8,128)S(1)} custom-call(f32[128,128]{1,0:T(8,128)S(1)} %cholesky.589), custom_call_target="Cholesky" | custom-call | tf_op jit(solution)/shard_map/jit(cholesky)/cholesky | solution.py:59
  190.0 11.8 %cholesky.487 = f32[128,128]{1,0:T(8,128)S(1)} custom-call(f32[128,128]{1,0:T(8,128)S(1)} %cholesky.594), custom_call_target="Cholesky" | custom-call | tf_op jit(solution)/shard_map/jit(cholesky)/cholesky | solution.py:59
  216.4 11.7 %cholesky.506 = f32[128,128]{1,0:T(8,128)S(1)} custom-call(f32[128,128]{1,0:T(8,128)S(1)} %cholesky.599), custom_call_target="Cholesky" | custom-call | tf_op jit(solution)/shard_map/jit(cholesky)/cholesky | solution.py:59
  229.4 10.0 %custom-call.67 = f32[1,128,128]{1,2,0:T(8,128)S(1)} custom-call(f32[1,128,128]{2,1,0:T(8,128)S(1)} %get-tuple-element.63), custom_call_target="InvertDiagBlocksLowerTriangular" | custom-call | tf_op jit(solution)/shard_map/jit(cholesky)/cholesky | solution.py:59
  242.7 11.7 %cholesky.526 = f32[128,128]{1,0:T(8,128)S(1)} custom-call(f32[128,128]{1,0:T(8,128)S(1)} %cholesky.604), custom_call_target="Cholesky" | custom-call | tf_op jit(solution)/shard_map/jit(cholesky)/cholesky | solution.py:59
  268.5 12.1 %cholesky.546 = f32[128,128]{1,0:T(8,128)S(1)} custom-call(f32[128,128]{1,0:T(8,128)S(1)} %cholesky.609), custom_call_target="Cholesky" | custom-call | tf_op jit(solution)/shard_map/jit(cholesky)/cholesky | solution.py:59
  294.3 11.7 %cholesky.564 = f32[128,128]{1,0:T(8,128)S(1)} custom-call(f32[128,128]{1,0:T(8,128)S(1)} %convolution_subtract_fusion.13), custom_call_target="Cholesky" | custom-call | tf_op jit(solution)/shard_map/jit(cholesky)/cholesky | solution.py:59
  319.7 23.2 %while.1 = (s32[]{:T(128)}, f32[1024,1024]{1,0:T(8,128)}, s32[8,2]{0,1:T(2,128)S(1)}, f32[8,128,128]{2,1,0:T(8,128)S(1)}, s32[]{:T(128)}) while((s32[]{:T(128)}, f32[1024,1024]{1,0:T(8,128)}, s32[8,2]{0,1:T(2,128)S(1)}, f32[8,128,128]{2,1,0:T(8,128)S(1)}, s32[]{:T(128)}) %tuple.67), condition=%wide.while_cond, body=%wide.while_body.sunk | while | flops 2 | bytes 131189 | solution.py:64
  342.9 78.8 %custom-call.70 = f32[8,128,128]{1,2,0:T(8,128)S(1)} custom-call(f32[8,128,128]{2,1,0:T(8,128)S(1)} %get-tuple-element.10), custom_call_target="InvertDiagBlocksLowerTriangular" | custom-call | tf_op jit(solution)/shard_map/jit(_solve_triangular)/triangular_solve | solution.py:64
  435.3 17.8 %collective-permute-done = f32[192,1024]{1,0:T(8,128)S(1)} collective-permute-done((f32[192,1024]{1,0:T(8,128)S(1)}, f32[192,1024]{1,0:T(8,128)S(1)}, u32[]{:S(2)}, u32[]{:S(2)}) %collective-permute-start) | collective-permute-done | bytes 786464 | tf_op jit(solution)/shard_map/ppermute | solution.py:67
  454.6 17.0 %collective-permute-done.1 = f32[192,1024]{1,0:T(8,128)S(1)} collective-permute-done((f32[192,1024]{1,0:T(8,128)S(1)}, f32[192,1024]{1,0:T(8,128)S(1)}, u32[]{:S(2)}, u32[]{:S(2)}) %collective-permute-start.1) | collective-permute-done | bytes 786464 | tf_op jit(solution)/shard_map/ppermute | solution.py:67
  473.0 17.3 %collective-permute-done.2 = f32[192,1024]{1,0:T(8,128)S(1)} collective-permute-done((f32[192,1024]{1,0:T(8,128)S(1)}, f32[192,1024]{1,0:T(8,128)S(1)}, u32[]{:S(2)}, u32[]{:S(2)}) %collective-permute-start.2) | collective-permute-done | bytes 786464 | tf_op jit(solution)/shard_map/ppermute | solution.py:67
  495.7 40.9 %reduce-scatter.3.cloned.1.call-done = f32[192,1024]{1,0:T(8,128)} async-done(((f32[768,1024]{1,0:T(8,128)}), f32[192,1024]{1,0:T(8,128)}) %reduce-scatter.3.cloned.1.call-update) | async-done | bytes 786448 | tf_op jit(solution)/shard_map/reduce_scatter | solution.py:52
  536.7 43.3 %all-gather.6.cloned.1.call-done = f32[768,1024]{1,0:T(8,128)} async-done(((f32[192,1024]{1,0:T(8,128)}), f32[768,1024]{1,0:T(8,128)}) %all-gather.6.cloned.1.call-update) | async-done | bytes 3145744 | tf_op jit(solution)/shard_map/all_gather | solution.py:53
  580.1 11.7 %bitcast_subtract_fusion = f32[768,768]{1,0:T(8,128)} fusion(f32[1,768,768]{2,1,0:T(8,128)S(1)} %copy-done.3, f32[768,1024]{1,0:T(8,128)} %all-gather.6.cloned.1.call-done, f32[1536,1024]{1,0:T(8,128)} %copy-done.1, s32[]{:T(128)S(6)} %select_n.56), kind=kOutput, calls=%fused_computation.16 | convolution fusion | flops 7248347136 | bytes 11010052 | tf_op jit(solution)/shard_map/dot_general | solution.py:73
  598.4 9.9 %fusion = f32[16,16,128,128]{3,0,2,1:T(8,128)S(1)} fusion(f32[16,128,6,128]{3,0,2,1:T(8,128)S(1)} %fusion.4, s32[6]{0:T(128)S(1)} %fusion.76), kind=kOutput, calls=%fused_computation.3 | convolution fusion | flops 301989984 | bytes 23068696 | tf_op jit(solution)/shard_map/pxcy,qc->pxqy/dot_general | solution.py:105
  608.3 11.2 %copy.25 = f32[256,8,16,128]{3,1,2,0:T(8,128)} copy(f32[256,8,16,128]{3,2,1,0:T(8,128)S(1)} %bitcast.142) | data formatting | bytes 33554432
  621.3 99.1 %reduce-scatter.5.cloned.1.call-done = f32[128,2048]{1,0:T(8,128)} async-done(((f32[2048,2048]{1,0:T(8,128)}), f32[128,2048]{1,0:T(8,128)}) %reduce-scatter.5.cloned.1.call-update) | async-done | bytes 1048592 | tf_op jit(solution)/shard_map/reduce_scatter | solution.py:106
  (134 shorter events, 174.5 us)
Async XLA Ops:
  7.2 50.6 %all-gather.8.cloned.1.call-start = ((), (), s32[]{:S(2)}) async-start(), calls=%async_computation.5 | async-start | bytes 2621440 | tf_op jit(solution)/shard_map/all_gather | solution.py:17
  22.3 71.7 %all-gather.10.cloned.1.call-start = ((), (), s32[]{:S(2)}) async-start(), calls=%async_computation.6 | async-start | bytes 2621440 | tf_op jit(solution)/shard_map/all_gather | solution.py:17
  35.9 500.6 %reduce-scatter.3.cloned.1.call-start = ((), (), s32[]{:S(2)}) async-start(), calls=%async_computation.2 | async-start | bytes 3932160 | tf_op jit(solution)/shard_map/reduce_scatter | solution.py:52
  107.9 1.9 copy-start
  313.0 108.7 %copy-start.5 = (f32[1,192,1024]{2,1,0:T(8,128)S(1)}, f32[1,192,1024]{2,1,0:T(8,128)}, u32[]{:S(2)}) copy-start(f32[1,192,1024]{2,1,0:T(8,128)} %param.6) | copy-start | bytes 2359300
  433.8 57.0 %copy-start.2 = (f32[1024,192]{0,1:T(8,128)}, f32[1024,192]{0,1:T(8,128)S(1)}, u32[]{:S(2)}) copy-start(f32[1024,192]{0,1:T(8,128)S(1)} %convolution_dynamic-update-slice_fusion.5) | copy-start | bytes 2359300
  433.8 19.4 %collective-permute-start = (f32[192,1024]{1,0:T(8,128)S(1)}, f32[192,1024]{1,0:T(8,128)S(1)}, u32[]{:S(2)}, u32[]{:S(2)}) collective-permute-start(f32[192,1024]{1,0:T(8,128)S(1)} %bitcast.146), channel_id=1, source_target_pairs={{0,1},{1,2},{2,3},{3,0},{4,5},{5,6},{6,7},{7,4},{8,9},{9,10},{10,1... | collective-permute-start | bytes 2359304 | tf_op jit(solution)/shard_map/ppermute | solution.py:67
  453.1 18.5 %collective-permute-start.1 = (f32[192,1024]{1,0:T(8,128)S(1)}, f32[192,1024]{1,0:T(8,128)S(1)}, u32[]{:S(2)}, u32[]{:S(2)}) collective-permute-start(f32[192,1024]{1,0:T(8,128)S(1)} %collective-permute-done), channel_id=1, source_target_pairs={{0,1},{1,2},{2,3},{3,0},{4,5},{5,6},{6,7},{7,4},{8,9},{9,10},{10,1... | collective-permute-start | bytes 2359304 | tf_op jit(solution)/shard_map/ppermute | solution.py:67
  471.6 18.7 %collective-permute-start.2 = (f32[192,1024]{1,0:T(8,128)S(1)}, f32[192,1024]{1,0:T(8,128)S(1)}, u32[]{:S(2)}, u32[]{:S(2)}) collective-permute-start(f32[192,1024]{1,0:T(8,128)S(1)} %collective-permute-done.1), channel_id=1, source_target_pairs={{0,1},{1,2},{2,3},{3,0},{4,5},{5,6},{6,7},{7,4},{8,9},{9,10},{10,1... | collective-permute-start | bytes 2359304 | tf_op jit(solution)/shard_map/ppermute | solution.py:67
  490.8 2.7 copy-start.1
  493.5 43.1 %copy-start.6 = (s32[16,24]{1,0:T(8,128)S(1)}, s32[16,24]{1,0:T(8,128)}, u32[]{:S(2)}) copy-start(s32[16,24]{1,0:T(8,128)} %param.9) | copy-start | bytes 4612
  493.5 86.6 %copy-start.3 = (f32[1,768,768]{2,1,0:T(8,128)S(1)}, f32[1,768,768]{2,1,0:T(8,128)}, u32[]{:S(2)}) copy-start(f32[1,768,768]{2,1,0:T(8,128)} %param.7) | copy-start | bytes 7077892
  495.6 84.5 %all-gather.6.cloned.1.call-start = ((), (), s32[]{:S(2)}) async-start(), calls=%async_computation.3 | async-start | bytes 3932160 | tf_op jit(solution)/shard_map/all_gather | solution.py:53
  536.6 183.8 %reduce-scatter.5.cloned.1.call-start = ((), (), s32[]{:S(2)}) async-start(), calls=%async_computation.4 | async-start | bytes 17825792 | tf_op jit(solution)/shard_map/reduce_scatter | solution.py:106
  619.5 100.9 %copy-start.4 = (f32[1,128,2048]{2,1,0:T(8,128)S(1)}, f32[1,128,2048]{2,1,0:T(8,128)}, u32[]{:S(2)}) copy-start(f32[1,128,2048]{2,1,0:T(8,128)} %param.8) | copy-start | bytes 3145732
Sparse Core Ops, SparseCore 0:
  22.4 35.3 all-gather.7
  59.6 34.4 all-gather.9
  495.7 40.7 reduce-scatter.2
  538.2 41.8 all-gather.5
  619.6 100.6 reduce-scatter.4
